TPU v7x, 512 devices: a whole 4x8x8 slice. The times are simulated.
512 devices in a mesh: island: 8 (over z_lo, x), replica: 8 (over z_hi, core), shard: 8 (over y).
Axes of the slice: x: 4, y: 8, z: 8 (z_hi: 4, z_lo: 2; z = z_hi * 2 + z_lo), core: 2. Of those that a mesh axis runs over, the one named last changes fastest.
Arguments:
- inputs: bfloat16 [2, 131072, 4096], P(None, ('island', 'replica', 'shard')), may hold values from -24 to 24
- targets: bfloat16 [2, 131072, 128], P(None, ('island', 'replica', 'shard')), may hold values from -6 to 6
- theta: float32 [4096, 128], P(('replica', 'shard')), may hold values from -6 to 6
- momentum: float32 [4096, 128], P(('replica', 'shard')), may hold values from -0.6 to 0.6
- first_moment: float32 [8, 4096, 128], P('island', ('replica', 'shard')), may hold values from -2 to 2
- second_moment: float32 [8, 4096, 128], P('island', ('replica', 'shard')), may hold values from 0.001 to 1
Outputs:
- theta_new: float32 [4096, 128], P(('replica', 'shard'))
- momentum_new: float32 [4096, 128], P(('replica', 'shard'))
- first_out: float32 [8, 4096, 128], P('island', ('replica', 'shard'))
- second_out: float32 [8, 4096, 128], P('island', ('replica', 'shard'))
All inputs are finite; a program needn't handle non-finite values.
Results may differ from a plain program's by a relative error of at most 0.0051.
Values may be sent and summed in bfloat16 or wider, within the bound.
A program may use at most 64 MiB of HBM per device.

v0:
```python
import math

import jax
import jax.numpy as jnp
from jax import lax
from jax.sharding import PartitionSpec as P

BETA_ONE = 0.9
BETA_TWO = 0.95
EPSILON = 1e-08
INNER_RATE = 0.05
DECAY = 0.1
OUTER_RATE = 0.7
OUTER_MOMENTUM = 0.9


def contract_tokens(columns, residual):
    return lax.dot_general(
        columns, residual, (((0,), (0,)), ((), ())), preferred_element_type=jnp.float32
    )


def per_device(inputs, targets, theta, momentum, first_moment, second_moment):
    tok_count = inputs.shape[1]
    feature_width = inputs.shape[2]
    replicas = lax.axis_size("replica")
    shards = lax.axis_size("shard")
    key_scale = feature_width ** (-0.5)
    grad_scale = 1.0 / math.sqrt(tok_count * replicas * shards)
    parameters = theta
    first = first_moment[0]
    second = second_moment[0]
    for inner_step in range(inputs.shape[0]):
        batch_inputs = inputs[inner_step]
        batch_targets = targets[inner_step]
        weights_half = parameters.astype(jnp.bfloat16)
        projected = jnp.dot(
            batch_inputs,
            lax.all_gather(weights_half, ("replica", "shard"), axis=0, tiled=True),
            preferred_element_type=jnp.float32,
        )
        residual = (projected * key_scale - batch_targets.astype(jnp.float32)).astype(jnp.bfloat16)
        gradient = lax.psum_scatter(
            contract_tokens(batch_inputs, residual) * grad_scale,
            ("replica", "shard"),
            scatter_dimension=0,
            tiled=True,
        )
        first = BETA_ONE * first + (1.0 - BETA_ONE) * gradient
        second = BETA_TWO * second + (1.0 - BETA_TWO) * gradient * gradient
        parameters = parameters - INNER_RATE * (
            first / (jnp.sqrt(second) + EPSILON) + DECAY * parameters
        )
    island_sum = lax.psum(parameters, "island")
    mean_params = island_sum / lax.axis_size("island")
    pseudo_grad = theta - mean_params
    momentum_new = OUTER_MOMENTUM * momentum + pseudo_grad
    theta_new = theta - OUTER_RATE * (pseudo_grad + OUTER_MOMENTUM * momentum_new)
    return (theta_new, momentum_new, first[None], second[None])


def solution(mesh):
    in_specs = (
        P(None, ("island", "replica", "shard"), None),
        P(None, ("island", "replica", "shard"), None),
        P(("replica", "shard"), None),
        P(("replica", "shard"), None),
        P("island", ("replica", "shard"), None),
        P("island", ("replica", "shard"), None),
    )
    out_specs = (
        P(("replica", "shard"), None),
        P(("replica", "shard"), None),
        P("island", ("replica", "shard"), None),
        P("island", ("replica", "shard"), None),
    )
    return jax.shard_map(
        per_device, mesh=mesh, in_specs=in_specs, out_specs=out_specs, check_vma=False
    )
```

profile of v0, /device:TPU:16, one launch (start us, length us, event | category | flops | bytes accessed | tf_op | source)
XLA Modules:
  0.0 534.1 jit_solution(7650945073667048646)
XLA Ops:
  7.2 0.0 all-gather.3.cloned.1.call-start
  7.2 1.4 convert_element_type.24
  8.6 0.0 all-gather.3.cloned.1.call-update
  8.6 0.0 reduce-scatter.7.cloned.1.call-start
  8.7 90.5 %all-gather.3.cloned.1.call-done = bf16[4096,128]{1,0:T(8,128)(2,1)} async-done(((bf16[64,128]{1,0:T(8,128)(2,1)}), bf16[4096,128]{1,0:T(8,128)(2,1)}) %all-gather.3.cloned.1.call-update) | async-done | bytes 1048592 | tf_op jit(solution)/shard_map/all_gather | solution.py:39
  99.1 3.7 fusion.1
  102.9 1.8 copy.40
  104.7 0.0 reduce-scatter.7.cloned.1.call-update
  104.8 0.0 all-gather.5.cloned.1.call-start
  104.8 148.7 %reduce-scatter.7.cloned.1.call-done = f32[64,128]{1,0:T(8,128)} async-done(((f32[4096,128]{1,0:T(8,128)}), f32[64,128]{1,0:T(8,128)}) %reduce-scatter.7.cloned.1.call-update) | async-done | bytes 32784 | tf_op jit(solution)/shard_map/reduce_scatter | solution.py:43
  253.5 0.0 copy-done
  253.5 1.4 fusion.48
  254.9 0.0 all-gather.5.cloned.1.call-update
  255.0 0.0 reduce-scatter.9.cloned.1.call-start
  255.0 0.0 slice-done
  255.0 0.1 copy.44
  255.1 82.2 %all-gather.5.cloned.1.call-done = bf16[4096,128]{1,0:T(8,128)(2,1)} async-done(((bf16[64,128]{1,0:T(8,128)(2,1)}), bf16[4096,128]{1,0:T(8,128)(2,1)}) %all-gather.5.cloned.1.call-update) | async-done | bytes 1048592 | tf_op jit(solution)/shard_map/all_gather | solution.py:39
  337.3 4.2 fusion
  341.5 1.8 copy.42
  343.4 0.0 reduce-scatter.9.cloned.1.call-update
  343.4 148.7 %reduce-scatter.9.cloned.1.call-done = f32[64,128]{1,0:T(8,128)} async-done(((f32[4096,128]{1,0:T(8,128)}), f32[64,128]{1,0:T(8,128)}) %reduce-scatter.9.cloned.1.call-update) | async-done | bytes 32784 | tf_op jit(solution)/shard_map/reduce_scatter | solution.py:43
  492.1 1.4 fusion.47
  493.5 33.4 %psum.7 = f32[64,128]{1,0:T(8,128)S(1)} all-reduce(f32[64,128]{1,0:T(8,128)S(1)} %get-tuple-element.15), channel_id=1, replica_groups=mesh['island'=8,'replica'=8,'shard'=8] {'island'}, use_global_device_ids=true, to_apply=%region_2.0 | all-reduce | flops 8192 | bytes 65536 | tf_op jit(solution)/shard_map/psum | solution.py:54
  527.0 0.6 multiply_subtract_fusion
  (10 shorter events, 0.0 us)
Async XLA Ops:
  7.2 92.0 %all-gather.3.cloned.1.call-start = ((), (), s32[]{:S(2)}) async-start(), calls=%async_computation.2 | async-start | bytes 1064960 | tf_op jit(solution)/shard_map/all_gather | solution.py:39
  8.6 244.9 %reduce-scatter.7.cloned.1.call-start = ((), (), s32[]{:S(2)}) async-start(), calls=%async_computation.4 | async-start | bytes 2129920 | tf_op jit(solution)/shard_map/reduce_scatter | solution.py:43
  104.7 148.8 %copy-start = (f32[64,128]{1,0:T(8,128)S(1)}, f32[64,128]{1,0:T(8,128)}, u32[]{:S(2)}) copy-start(f32[64,128]{1,0:T(8,128)} %param.8) | copy-start | bytes 98308
  104.7 148.8 %copy-start.1 = (f32[1,64,128]{2,1,0:T(8,128)S(1)}, f32[1,64,128]{2,1,0:T(8,128)}, u32[]{:S(2)}) copy-start(f32[1,64,128]{2,1,0:T(8,128)} %param.10) | copy-start | bytes 98308
  104.7 148.8 %copy-start.2 = (f32[1,64,128]{2,1,0:T(8,128)S(1)}, f32[1,64,128]{2,1,0:T(8,128)}, u32[]{:S(2)}) copy-start(f32[1,64,128]{2,1,0:T(8,128)} %param.11) | copy-start | bytes 98308
  104.7 150.3 %slice-start = ((bf16[2,256,128]{2,1,0:T(8,128)(2,1)}), bf16[1,256,128]{2,1,0:T(8,128)(2,1)S(1)}, s32[]{:S(2)}) async-start(bf16[2,256,128]{2,1,0:T(8,128)(2,1)} %param.7), calls=%async_computation.6 | async-start | bytes 131072 | tf_op jit(solution)/shard_map/slice | solution.py:35
  104.8 232.6 %all-gather.5.cloned.1.call-start = ((), (), s32[]{:S(2)}) async-start(), calls=%async_computation.3 | async-start | bytes 1064960 | tf_op jit(solution)/shard_map/all_gather | solution.py:39
  255.0 237.2 %reduce-scatter.9.cloned.1.call-start = ((), (), s32[]{:S(2)}) async-start(), calls=%async_computation.5 | async-start | bytes 2129920 | tf_op jit(solution)/shard_map/reduce_scatter | solution.py:43
  343.3 148.8 %copy-start.3 = (f32[64,128]{1,0:T(8,128)S(1)}, f32[64,128]{1,0:T(8,128)}, u32[]{:S(2)}) copy-start(f32[64,128]{1,0:T(8,128)} %reduce-scatter.7.cloned.1.call-done) | copy-start | bytes 98308
  343.4 183.6 %copy-start.4 = (f32[64,128]{1,0:T(8,128)S(1)}, f32[64,128]{1,0:T(8,128)}, u32[]{:S(2)}) copy-start(f32[64,128]{1,0:T(8,128)} %param.9) | copy-start | bytes 98308
Sparse Core Ops, SparseCore 0:
  11.9 87.2 all-gather.2
  104.9 148.6 reduce-scatter.6
  257.9 79.3 all-gather.4
  343.5 148.5 reduce-scatter.8
where the time goes:
time: 534 us
  waiting for transfers between devices  470 us (88%)
  blocking collectives  33.4 us (6%)
  between operations  13.8 us (3%)
  matrix products  7.92 us (1%)
    reduce_scatter x2, waiting for transfers between devices, per_device(): lax.psum_scatter(contract_tokens(batch_inputs, residual) * grad_scale, ('...  297 us
    all_gather x2, waiting for transfers between devices, per_device(): lax.all_gather(weights_half, ('replica', 'shard'), axis=0, tiled=True)  173 us
    psum x1, blocking collectives, per_device(): island_sum = lax.psum(parameters, 'island')  33.4 us
  transfers between devices with their start and end apart: 4, of which 4 were waited for; matrix products, arithmetic and copies ran while one was open for 0% of the time, Pallas kernels for 0%

commit v1 on v0

v1 whole, which is shorter than its diff:
```python
import functools
import math

import jax
import jax.numpy as jnp
from jax import lax
from jax.experimental import pallas as pl
from jax.experimental.pallas import tpu as pltpu
from jax.sharding import PartitionSpec as P

BETA_ONE = 0.9
BETA_TWO = 0.95
EPSILON = 1e-08
INNER_RATE = 0.05
DECAY = 0.1
OUTER_RATE = 0.7
OUTER_MOMENTUM = 0.9

MESH = pl.DeviceIdType.MESH
F32 = jnp.float32
BF16 = jnp.bfloat16


def kernel(
    sizes,
    x_hbm, t_hbm, theta_hbm, momentum_hbm, first_hbm, second_hbm,
    theta_out, momentum_out, first_out, second_out,
    xs, xt, ts, state, weights, part_out, part_in,
    grads, near_a, sum_a, far_a, near_b, sum_b, far_b,
    pool_out, pool_in,
    x_local, x_send, x_recv, t_sems, state_sems, out_sems,
    part_send, part_recv, send, recv, pool_send, pool_recv,
):
    steps, depths, rows, islands = sizes
    island = lax.axis_index("island")
    replica = lax.axis_index("replica")
    row = lax.axis_index("shard")
    depth, core = replica // 2, replica % 2
    tokens = x_hbm.shape[1]
    width = xs.shape[3]
    head = t_hbm.shape[2]
    half = weights.shape[4]
    key_scale = (depths * 2 * width) ** (-0.5)
    grad_scale = 1.0 / math.sqrt(tokens * 2 * depths * rows)

    def over_rows(offset):
        return {"shard": (row + offset) % rows}

    def over_depths(offset):
        return {"replica": (depth + offset) % depths * 2 + core}

    sibling = {"replica": depth * 2 + 1 - core}

    def over_islands(offset):
        return {"island": (island + offset) % islands}

    def remote(source, target, send_sem, recv_sem, where):
        return pltpu.make_async_remote_copy(
            src_ref=source, dst_ref=target, send_sem=send_sem, recv_sem=recv_sem,
            device_id=where, device_id_type=MESH,
        )

    barrier = pltpu.get_barrier_semaphore()
    greeted = [over_rows(k) for k in range(1, rows)] + [over_depths(k) for k in range(1, depths)]
    greeted += [sibling] + [over_islands(k) for k in range(1, islands)]
    for where in greeted:
        pl.semaphore_signal(barrier, inc=1, device_id=where, device_id_type=MESH)

    def load(k, source):
        return pltpu.make_async_copy(source, state.at[k], state_sems.at[k])

    loads = [load(0, theta_hbm), load(1, momentum_hbm), load(2, first_hbm), load(3, second_hbm)]
    loads[0].start()
    own_tokens = pl.ds(pl.multiple_of(core * tokens, tokens), tokens)

    def x_columns(z, which):
        return pl.ds(pl.multiple_of((z * 2 + which) * width, width), width)

    def x_mine(s, z):
        return pltpu.make_async_copy(
            x_hbm.at[s, :, x_columns(z, core)], xs.at[s, z, own_tokens], x_local.at[s, z]
        )

    def x_theirs(s, z):
        return remote(
            x_hbm.at[s, :, x_columns(z, 1 - core)], xs.at[s, z, own_tokens],
            x_send.at[s, z], x_recv.at[s, z], sibling,
        )

    t_mine = pltpu.make_async_copy(t_hbm, ts.at[:, own_tokens], t_sems.at[0])
    t_theirs = remote(t_hbm, ts.at[:, own_tokens], t_sems.at[1], t_sems.at[2], sibling)
    for z in range(depths):
        x_mine(0, z).start()
    t_mine.start()
    for k in (1, 2, 3):
        loads[k].start()
    for s in range(1, steps):
        for z in range(depths):
            x_mine(s, z).start()

    def gather_near_a(s, k):
        block = weights.at[s, depth, row, 0]
        return remote(block, block, send.at[s, 0, k - 1], recv.at[s, 0, k - 1], over_rows(k))

    def gather_near_b(s, k):
        block, i = weights.at[s, depth, row, 1], rows + k - 2
        return remote(block, block, send.at[s, 0, i], recv.at[s, 0, i], over_depths(k))

    def gather_far_a(s, k):
        block, i = weights.at[s, depth, :, 0], rows + depths + k - 3
        return remote(block, block, send.at[s, 0, i], recv.at[s, 0, i], over_depths(k))

    def gather_far_b(s, k):
        block, i = weights.at[s, :, row, 1], rows + 2 * depths + k - 4
        return remote(block, block, send.at[s, 0, i], recv.at[s, 0, i], over_rows(k))

    def scatter_near_a(s, k):
        block, i = grads.at[s, (depth + k) % depths, :, 0], k - 1
        return remote(block, near_a.at[s, k - 1], send.at[s, 1, i], recv.at[s, 1, i], over_depths(k))

    def scatter_near_b(s, k):
        block, i = grads.at[s, :, (row + k) % rows, 1], depths + k - 2
        return remote(block, near_b.at[s, k - 1], send.at[s, 1, i], recv.at[s, 1, i], over_rows(k))

    def scatter_far_a(s, k):
        block, i = sum_a.at[s, (row + k) % rows], depths + rows + k - 3
        return remote(block, far_a.at[s, k - 1], send.at[s, 1, i], recv.at[s, 1, i], over_rows(k))

    def scatter_far_b(s, k):
        block, i = sum_b.at[s, (depth + k) % depths], depths + 2 * rows + k - 4
        return remote(block, far_b.at[s, k - 1], send.at[s, 1, i], recv.at[s, 1, i], over_depths(k))

    def over(copies_of, s, count):
        return [copies_of(s, k) for k in range(1, count)]

    def start(copies):
        for copy in copies:
            copy.start()

    def arrive(copies):
        for copy in copies:
            copy.wait_recv()

    def transposed(s):
        for z in range(depths):
            xt[s, z] = xs[s, z].T

    loads[0].wait()
    weights[0, depth, row] = state[0].astype(BF16)
    pl.semaphore_wait(barrier, len(greeted))

    for s in range(steps):
        start(over(gather_near_b, s, depths) + over(gather_near_a, s, rows))
        if s == 0:
            for z in range(depths):
                x_theirs(0, z).start()
            t_theirs.start()
        arrive(over(gather_near_b, s, depths))
        start(over(gather_far_b, s, rows))
        arrive(over(gather_near_a, s, rows))
        start(over(gather_far_a, s, depths))
        if s == 0:
            for later in range(1, steps):
                for z in range(depths):
                    x_theirs(later, z).start()
            t_mine.wait()
            t_theirs.wait_recv()
        for z in range(depths):
            x_mine(s, z).wait()
            x_theirs(s, z).wait_recv()
        transposed(s)
        arrive(over(gather_far_b, s, rows) + over(gather_far_a, s, depths))

        def part(p):
            block = part_out.at[s, pl.ds(p * tokens, tokens)]
            return remote(
                block, part_in.at[s, pl.ds(p * tokens, tokens)],
                part_send.at[s, p], part_recv.at[s, p], sibling,
            )

        for p in range(2):
            total = jnp.zeros((tokens, head), F32)
            for z in range(depths):
                total += jnp.dot(
                    xs[s, z, p * tokens:(p + 1) * tokens],
                    weights[s, z].reshape(width, head),
                    preferred_element_type=F32,
                )
            part_out[s, p * tokens:(p + 1) * tokens] = total
            part(p).start()
        arrive([part(0), part(1)])
        projected = (part_out[s] + part_in[s]) * key_scale
        residual = (projected - ts[s].astype(F32)).astype(BF16)

        for z in range(depths):
            gradient = jnp.dot(xt[s, z], residual, preferred_element_type=F32) * grad_scale
            grads[s, z] = gradient.astype(BF16).reshape(rows, 2, half, head)
        start(over(scatter_near_a, s, depths) + over(scatter_near_b, s, rows))
        arrive(over(scatter_near_a, s, depths))
        total_a = grads[s, depth, :, 0].astype(F32)
        for k in range(depths - 1):
            total_a += near_a[s, k].astype(F32)
        sum_a[s] = total_a.astype(BF16)
        start(over(scatter_far_a, s, rows))
        arrive(over(scatter_near_b, s, rows))
        total_b = grads[s, :, row, 1].astype(F32)
        for k in range(rows - 1):
            total_b += near_b[s, k].astype(F32)
        sum_b[s] = total_b.astype(BF16)
        start(over(scatter_far_b, s, depths))

        if s == 0:
            for k in (1, 2, 3):
                loads[k].wait()

        def update(part_index, gradient):
            parameters = state[0 if s == 0 else 4, part_index]
            first = BETA_ONE * state[2, part_index] + (1.0 - BETA_ONE) * gradient
            second = BETA_TWO * state[3, part_index] + (1.0 - BETA_TWO) * gradient * gradient
            parameters = parameters - INNER_RATE * (
                first / (jnp.sqrt(second) + EPSILON) + DECAY * parameters
            )
            state[2, part_index] = first
            state[3, part_index] = second
            state[4, part_index] = parameters
            if s < steps - 1:
                weights[s + 1, depth, row, part_index] = parameters.astype(BF16)

        arrive(over(scatter_far_a, s, rows))
        total_a = sum_a[s, row].astype(F32)
        for k in range(rows - 1):
            total_a += far_a[s, k].astype(F32)
        update(0, total_a)
        arrive(over(scatter_far_b, s, depths))
        total_b = sum_b[s, depth].astype(F32)
        for k in range(depths - 1):
            total_b += far_b[s, k].astype(F32)
        update(1, total_b)

    moved = state[0] - state[4]
    pool_out[...] = moved

    def pool(k):
        return remote(
            pool_out, pool_in.at[k - 1], pool_send.at[k - 1], pool_recv.at[k - 1], over_islands(k)
        )

    pools = [pool(k) for k in range(1, islands)]
    start(pools)
    stores = [
        pltpu.make_async_copy(state.at[2], first_out, out_sems.at[2]),
        pltpu.make_async_copy(state.at[3], second_out, out_sems.at[3]),
    ]
    start(stores)
    for z in range(depths):
        for s in range(steps):
            x_theirs(s, z).wait_send()
    t_theirs.wait_send()
    for s in range(steps):
        for p in range(2):
            block = part_out.at[s, pl.ds(p * tokens, tokens)]
            remote(block, block, part_send.at[s, p], part_recv.at[s, p], sibling).wait_send()
        for copies_of, count in (
            (gather_near_a, rows), (gather_near_b, depths), (gather_far_a, depths), (gather_far_b, rows),
            (scatter_near_a, depths), (scatter_near_b, rows), (scatter_far_a, rows), (scatter_far_b, depths),
        ):
            for copy in over(copies_of, s, count):
                copy.wait_send()
    arrive(pools)
    total = moved
    for k in range(islands - 1):
        total += pool_in[k]
    pseudo_grad = total / islands
    momentum_new = OUTER_MOMENTUM * state[1] + pseudo_grad
    state[1] = momentum_new
    state[4] = state[0] - OUTER_RATE * (pseudo_grad + OUTER_MOMENTUM * momentum_new)
    last = [
        pltpu.make_async_copy(state.at[4], theta_out, out_sems.at[0]),
        pltpu.make_async_copy(state.at[1], momentum_out, out_sems.at[1]),
    ]
    start(last)
    for copy in pools:
        copy.wait_send()
    for copy in stores + last:
        copy.wait()


def per_device(inputs, targets, theta, momentum, first_moment, second_moment):
    steps, tokens, _ = inputs.shape
    block, head = theta.shape
    islands = lax.axis_size("island")
    depths, rows = lax.axis_size("replica") // 2, lax.axis_size("shard")
    half, width = block // 2, rows * block
    split = (2, half, head)
    copies = 2 * (rows + depths - 2)
    dma = pltpu.SemaphoreType.DMA
    anywhere = pl.BlockSpec(memory_space=pl.ANY)
    vmem = pltpu.VMEM
    outs = pl.pallas_call(
        functools.partial(kernel, (steps, depths, rows, islands)),
        out_shape=[jax.ShapeDtypeStruct(split, F32)] * 4,
        in_specs=[anywhere] * 6,
        out_specs=[anywhere] * 4,
        scratch_shapes=[
            vmem((steps, depths, 2 * tokens, width), BF16),
            vmem((steps, depths, width, 2 * tokens), BF16),
            vmem((steps, 2 * tokens, head), BF16),
            vmem((5,) + split, F32),
            vmem((steps, depths, rows) + split, BF16),
            vmem((steps, 2 * tokens, head), F32),
            vmem((steps, 2 * tokens, head), F32),
            vmem((steps, depths, rows) + split, BF16),
            vmem((steps, depths - 1, rows, half, head), BF16),
            vmem((steps, rows, half, head), BF16),
            vmem((steps, rows - 1, half, head), BF16),
            vmem((steps, rows - 1, depths, half, head), BF16),
            vmem((steps, depths, half, head), BF16),
            vmem((steps, depths - 1, half, head), BF16),
            vmem(split, F32),
            vmem((islands - 1,) + split, F32),
            dma((steps, depths)), dma((steps, depths)), dma((steps, depths)),
            dma((3,)), dma((4,)), dma((4,)),
            dma((steps, 2)), dma((steps, 2)),
            dma((steps, 2, copies)), dma((steps, 2, copies)),
            dma((islands - 1,)), dma((islands - 1,)),
        ],
        compiler_params=pltpu.CompilerParams(
            collective_id=0, has_side_effects=True, vmem_limit_bytes=40 * 1024 * 1024
        ),
    )(
        inputs, targets, theta.reshape(split), momentum.reshape(split),
        first_moment.reshape(split), second_moment.reshape(split),
    )
    theta_new, momentum_new, first, second = [out.reshape(block, head) for out in outs]
    return (theta_new, momentum_new, first[None], second[None])


def solution(mesh):
    in_specs = (
        P(None, ("island", "replica", "shard"), None),
        P(None, ("island", "replica", "shard"), None),
        P(("replica", "shard"), None),
        P(("replica", "shard"), None),
        P("island", ("replica", "shard"), None),
        P("island", ("replica", "shard"), None),
    )
    out_specs = (
        P(("replica", "shard"), None),
        P(("replica", "shard"), None),
        P("island", ("replica", "shard"), None),
        P("island", ("replica", "shard"), None),
    )
    return jax.shard_map(
        per_device, mesh=mesh, in_specs=in_specs, out_specs=out_specs, check_vma=False
    )
```

time: 534 us -> 89.1 us (0.17)
  the two profiles are of different devices: /device:TPU:16 before, /device:TPU:1 now
where the time goes in v1:
time: 89.1 us; the launch traced here: 88.7 us
  Pallas kernels  79.5 us (89%)
  local copies, waits for them, and re-layouts  8.57 us (10%)
    pallas_call x1, Pallas kernels, per_device(): pl.pallas_call(functools.partial(kernel, (steps, depths, rows, islands)),...  79.5 us
    unnamed x16, local copies, waits for them, and re-layouts  8.57 us

profile of v1, /device:TPU:1, one launch (start us, length us, event | category | flops | bytes accessed | tf_op | source)
XLA Modules:
  0.0 88.7 jit_solution(5458322887195306182)
XLA Ops:
  0.6 0.0 copy-start
  0.6 2.2 %copy-done = bf16[2,256,4096]{2,1,0:T(8,128)(2,1)S(1)} copy-done((bf16[2,256,4096]{2,1,0:T(8,128)(2,1)S(1)}, bf16[2,256,4096]{2,1,0:T(8,128)(2,1)}, u32[]{:S(2)}) %copy-start) | copy-done | bytes 4194328
  2.8 0.0 copy-start.1
  2.8 0.9 %copy-done.1 = bf16[2,256,128]{2,1,0:T(8,128)(2,1)S(1)} copy-done((bf16[2,256,128]{2,1,0:T(8,128)(2,1)S(1)}, bf16[2,256,128]{2,1,0:T(8,128)(2,1)}, u32[]{:S(2)}) %copy-start.1) | copy-done | bytes 131096
  3.7 0.0 copy-start.2
  3.7 0.8 copy-done.2
  4.5 0.0 copy-start.3
  4.5 0.8 copy-done.3
  5.2 0.0 copy-start.4
  5.2 0.8 copy-done.4
  6.0 0.0 copy-start.5
  6.0 0.8 copy-done.5
  6.8 79.5 %shard_map.93 = (f32[2,32,128]{2,1,0:T(8,128)S(1)}, f32[2,32,128]{2,1,0:T(8,128)S(1)}, f32[2,32,128]{2,1,0:T(8,128)S(1)}, f32[2,32,128]{2,1,0:T(8,128)S(1)}) custom-call(bf16[2,256,4096]{2,1,0:T(8,128)(2,1)S(1)} %copy-done, bf16[2,256,128]{2,1,0:T(8,128)(2,1)S(1)} %copy-done.1, f32[2,32,128]{2,1,0:T(8,128)S(1)} %bitcast.8, f32[2,32,128]{2,1,0:T(8,128)S(1)} %bitcast.9, ...), custom_call_target="tpu_custom_call" | custom-call | tf_op jit(solution)/shard_map/pallas_call | solution.py:299
  86.2 0.6 copy.14
  86.8 0.6 copy.15
  87.5 0.6 copy.16
  88.1 0.6 copy.17
Async XLA Ops:
  0.6 2.2 %copy-start = (bf16[2,256,4096]{2,1,0:T(8,128)(2,1)S(1)}, bf16[2,256,4096]{2,1,0:T(8,128)(2,1)}, u32[]{:S(2)}) copy-start(bf16[2,256,4096]{2,1,0:T(8,128)(2,1)} %x_hbm.1) | copy-start | bytes 12582916
  2.8 0.9 %copy-start.1 = (bf16[2,256,128]{2,1,0:T(8,128)(2,1)S(1)}, bf16[2,256,128]{2,1,0:T(8,128)(2,1)}, u32[]{:S(2)}) copy-start(bf16[2,256,128]{2,1,0:T(8,128)(2,1)} %t_hbm.1) | copy-start | bytes 393220
  3.7 0.8 copy-start.2
  4.5 0.8 copy-start.3
  5.2 0.8 copy-start.4
  6.0 0.8 copy-start.5

commit v2 on v1

--- a/solution.py
+++ b/solution.py
@@ -24,11 +24,11 @@
 def kernel(
     sizes,
     x_hbm, t_hbm, theta_hbm, momentum_hbm, first_hbm, second_hbm,
-    theta_out, momentum_out, first_out, second_out,
-    xs, xt, ts, state, weights, part_out, part_in,
+    result,
+    xs, ts, state, weights, part_out, part_in,
     grads, near_a, sum_a, far_a, near_b, sum_b, far_b,
     pool_out, pool_in,
-    x_local, x_send, x_recv, t_sems, state_sems, out_sems,
+    x_local, x_send, x_recv, t_sems, state_sems,
     part_send, part_recv, send, recv, pool_send, pool_recv,
 ):
     steps, depths, rows, islands = sizes
@@ -98,40 +98,81 @@
         for z in range(depths):
             x_mine(s, z).start()
 
-    def gather_near_a(s, k):
-        block = weights.at[s, depth, row, 0]
+    def gather_rows(s, k):
+        block = weights.at[s, depth, row]
         return remote(block, block, send.at[s, 0, k - 1], recv.at[s, 0, k - 1], over_rows(k))
 
-    def gather_near_b(s, k):
-        block, i = weights.at[s, depth, row, 1], rows + k - 2
+    def gather_depths(s, k):
+        block, i = weights.at[s, depth, row], rows + k - 2
         return remote(block, block, send.at[s, 0, i], recv.at[s, 0, i], over_depths(k))
 
-    def gather_far_a(s, k):
-        block, i = weights.at[s, depth, :, 0], rows + depths + k - 3
-        return remote(block, block, send.at[s, 0, i], recv.at[s, 0, i], over_depths(k))
-
-    def gather_far_b(s, k):
-        block, i = weights.at[s, :, row, 1], rows + 2 * depths + k - 4
-        return remote(block, block, send.at[s, 0, i], recv.at[s, 0, i], over_rows(k))
-
-    def scatter_near_a(s, k):
-        block, i = grads.at[s, (depth + k) % depths, :, 0], k - 1
-        return remote(block, near_a.at[s, k - 1], send.at[s, 1, i], recv.at[s, 1, i], over_depths(k))
-
-    def scatter_near_b(s, k):
-        block, i = grads.at[s, :, (row + k) % rows, 1], depths + k - 2
-        return remote(block, near_b.at[s, k - 1], send.at[s, 1, i], recv.at[s, 1, i], over_rows(k))
+    relay_a, relay_b = rows + depths - 2, rows + depths - 1
+
+    def on_from_rows(s, k):
+        gather_rows(s, k).wait_recv()
+        block = weights.at[s, depth, (row + rows - k) % rows, 0]
+        for m in far_depths:
+            remote(block, block, send.at[s, 0, relay_a], recv.at[s, 0, relay_a], over_depths(m)).start()
+
+    def on_from_depths(s, k):
+        gather_depths(s, k).wait_recv()
+        block = weights.at[s, (depth + depths - k) % depths, row, 1]
+        for m in far_rows:
+            remote(block, block, send.at[s, 0, relay_b], recv.at[s, 0, relay_b], over_rows(m)).start()
+
+    def relayed(s):
+        block = weights.at[s, 0:depths - 1, 0:rows - 1, 0]
+        return [
+            remote(block, block, send.at[s, 0, i], recv.at[s, 0, i], sibling) for i in (relay_a, relay_b)
+        ]
+
+    def scatter_depths(s, j, k):
+        return remote(
+            grads.at[s, (depth + k) % depths, (row + j) % rows, 0], near_a.at[s, k - 1, j],
+            send.at[s, 1, 0], recv.at[s, 1, j], over_depths(k),
+        )
+
+    def scatter_rows(s, j, k):
+        return remote(
+            grads.at[s, (depth + j) % depths, (row + k) % rows, 1], near_b.at[s, k - 1, j],
+            send.at[s, 1, 1], recv.at[s, 1, rows + j], over_rows(k),
+        )
 
     def scatter_far_a(s, k):
-        block, i = sum_a.at[s, (row + k) % rows], depths + rows + k - 3
-        return remote(block, far_a.at[s, k - 1], send.at[s, 1, i], recv.at[s, 1, i], over_rows(k))
+        i = rows + depths + k - 1
+        return remote(sum_a.at[s, k], far_a.at[s, k - 1], send.at[s, 1, i], recv.at[s, 1, i], over_rows(k))
 
     def scatter_far_b(s, k):
-        block, i = sum_b.at[s, (depth + k) % depths], depths + 2 * rows + k - 4
-        return remote(block, far_b.at[s, k - 1], send.at[s, 1, i], recv.at[s, 1, i], over_depths(k))
-
-    def over(copies_of, s, count):
-        return [copies_of(s, k) for k in range(1, count)]
+        i = 2 * rows + depths + k - 2
+        return remote(sum_b.at[s, k], far_b.at[s, k - 1], send.at[s, 1, i], recv.at[s, 1, i], over_depths(k))
+
+    def combine_a(s, j):
+        block = near_a.at[s, :, j]
+        remote(block, block, send.at[s, 1, 0], recv.at[s, 1, j], sibling).wait_recv()
+        total = grads[s, depth, (row + j) % rows, 0].astype(F32)
+        for k in range(depths - 1):
+            total += near_a[s, k, j].astype(F32)
+        if j == 0:
+            return total
+        sum_a[s, j] = total.astype(BF16)
+        scatter_far_a(s, j).start()
+
+    def combine_b(s, j):
+        block = near_b.at[s, :, j]
+        remote(block, block, send.at[s, 1, 1], recv.at[s, 1, rows + j], sibling).wait_recv()
+        total = grads[s, (depth + j) % depths, row, 1].astype(F32)
+        for k in range(rows - 1):
+            total += near_b[s, k, j].astype(F32)
+        if j == 0:
+            return total
+        sum_b[s, j] = total.astype(BF16)
+        scatter_far_b(s, j).start()
+
+    def far_first(count):
+        return sorted(range(1, count), key=lambda k: (-min(k, count - k), k))
+
+    far_rows, far_depths = far_first(rows), far_first(depths)
+    near_rows, near_depths = far_rows[::-1], far_depths[::-1]
 
     def start(copies):
         for copy in copies:
@@ -141,24 +182,19 @@
         for copy in copies:
             copy.wait_recv()
 
-    def transposed(s):
-        for z in range(depths):
-            xt[s, z] = xs[s, z].T
-
     loads[0].wait()
     weights[0, depth, row] = state[0].astype(BF16)
     pl.semaphore_wait(barrier, len(greeted))
 
     for s in range(steps):
-        start(over(gather_near_b, s, depths) + over(gather_near_a, s, rows))
+        start([gather_depths(s, k) for k in near_depths] + [gather_rows(s, k) for k in near_rows])
         if s == 0:
             for z in range(depths):
                 x_theirs(0, z).start()
             t_theirs.start()
-        arrive(over(gather_near_b, s, depths))
-        start(over(gather_far_b, s, rows))
-        arrive(over(gather_near_a, s, rows))
-        start(over(gather_far_a, s, depths))
+        hops = [(min(k, rows - k), 0, k) for k in near_rows] + [(2 * min(k, depths - k), 1, k) for k in near_depths]
+        for _, along, k in sorted(hops):
+            (on_from_depths if along else on_from_rows)(s, k)
         if s == 0:
             for later in range(1, steps):
                 for z in range(depths):
@@ -168,8 +204,7 @@
         for z in range(depths):
             x_mine(s, z).wait()
             x_theirs(s, z).wait_recv()
-        transposed(s)
-        arrive(over(gather_far_b, s, rows) + over(gather_far_a, s, depths))
+        arrive(relayed(s))
 
         def part(p):
             block = part_out.at[s, pl.ds(p * tokens, tokens)]
@@ -192,26 +227,24 @@
         projected = (part_out[s] + part_in[s]) * key_scale
         residual = (projected - ts[s].astype(F32)).astype(BF16)
 
-        for z in range(depths):
-            gradient = jnp.dot(xt[s, z], residual, preferred_element_type=F32) * grad_scale
-            grads[s, z] = gradient.astype(BF16).reshape(rows, 2, half, head)
-        start(over(scatter_near_a, s, depths) + over(scatter_near_b, s, rows))
-        arrive(over(scatter_near_a, s, depths))
-        total_a = grads[s, depth, :, 0].astype(F32)
-        for k in range(depths - 1):
-            total_a += near_a[s, k].astype(F32)
-        sum_a[s] = total_a.astype(BF16)
-        start(over(scatter_far_a, s, rows))
-        arrive(over(scatter_near_b, s, rows))
-        total_b = grads[s, :, row, 1].astype(F32)
-        for k in range(rows - 1):
-            total_b += near_b[s, k].astype(F32)
-        sum_b[s] = total_b.astype(BF16)
-        start(over(scatter_far_b, s, depths))
-
+        early, late = far_rows[:rows // 2 - 1], far_rows[rows // 2 - 1:] + [0]
+        for z in far_depths + [0]:
+            at = (depth + z) % depths
+            gradient = lax.dot_general(
+                xs[s, at], residual, (((0,), (0,)), ((), ())), preferred_element_type=F32
+            ) * grad_scale
+            grads[s, at] = gradient.astype(BF16).reshape(rows, 2, half, head)
+            if z > 0:
+                start([scatter_depths(s, j, z) for j in early])
+            start([scatter_rows(s, z, k) for k in far_rows])
+        start([scatter_depths(s, j, z) for j in late for z in far_depths])
         if s == 0:
             for k in (1, 2, 3):
                 loads[k].wait()
+        order = [(min(j, rows - j), 0, j) for j in range(rows)] + [(2 * min(j, depths - j), 1, j) for j in range(depths)]
+        totals = {}
+        for _, along, j in sorted(order, reverse=True):
+            totals[along] = (combine_b if along else combine_a)(s, j)
 
         def update(part_index, gradient):
             parameters = state[0 if s == 0 else 4, part_index]
@@ -226,19 +259,17 @@
             if s < steps - 1:
                 weights[s + 1, depth, row, part_index] = parameters.astype(BF16)
 
-        arrive(over(scatter_far_a, s, rows))
-        total_a = sum_a[s, row].astype(F32)
-        for k in range(rows - 1):
-            total_a += far_a[s, k].astype(F32)
-        update(0, total_a)
-        arrive(over(scatter_far_b, s, depths))
-        total_b = sum_b[s, depth].astype(F32)
-        for k in range(depths - 1):
-            total_b += far_b[s, k].astype(F32)
-        update(1, total_b)
+        for k in near_rows:
+            scatter_far_a(s, k).wait_recv()
+            totals[0] += far_a[s, k - 1].astype(F32)
+        update(0, totals[0])
+        for k in near_depths:
+            scatter_far_b(s, k).wait_recv()
+            totals[1] += far_b[s, k - 1].astype(F32)
+        update(1, totals[1])
 
     moved = state[0] - state[4]
-    pool_out[...] = moved
+    pool_out[...] = moved.astype(BF16)
 
     def pool(k):
         return remote(
@@ -247,10 +278,11 @@
 
     pools = [pool(k) for k in range(1, islands)]
     start(pools)
-    stores = [
-        pltpu.make_async_copy(state.at[2], first_out, out_sems.at[2]),
-        pltpu.make_async_copy(state.at[3], second_out, out_sems.at[3]),
-    ]
+
+    def store(k, source):
+        return pltpu.make_async_copy(source, result.at[k], state_sems.at[k])
+
+    stores = [store(2, state.at[2]), store(3, state.at[3])]
     start(stores)
     for z in range(depths):
         for s in range(steps):
@@ -260,28 +292,40 @@
         for p in range(2):
             block = part_out.at[s, pl.ds(p * tokens, tokens)]
             remote(block, block, part_send.at[s, p], part_recv.at[s, p], sibling).wait_send()
-        for copies_of, count in (
-            (gather_near_a, rows), (gather_near_b, depths), (gather_far_a, depths), (gather_far_b, rows),
-            (scatter_near_a, depths), (scatter_near_b, rows), (scatter_far_a, rows), (scatter_far_b, depths),
-        ):
-            for copy in over(copies_of, s, count):
-                copy.wait_send()
+        for k in near_rows:
+            gather_rows(s, k).wait_send()
+            scatter_far_a(s, k).wait_send()
+        for k in near_depths:
+            gather_depths(s, k).wait_send()
+            scatter_far_b(s, k).wait_send()
+        for copy in relayed(s):
+            copy.wait_send()
+        block = grads.at[s, 0:depths - 1, :, 0]
+        remote(block, block, send.at[s, 1, 0], recv.at[s, 1, 0], sibling).wait_send()
+        block = grads.at[s, :, 0:rows - 1, 1]
+        remote(block, block, send.at[s, 1, 1], recv.at[s, 1, 0], sibling).wait_send()
     arrive(pools)
     total = moved
     for k in range(islands - 1):
-        total += pool_in[k]
+        total += pool_in[k].astype(F32)
     pseudo_grad = total / islands
     momentum_new = OUTER_MOMENTUM * state[1] + pseudo_grad
     state[1] = momentum_new
     state[4] = state[0] - OUTER_RATE * (pseudo_grad + OUTER_MOMENTUM * momentum_new)
-    last = [
-        pltpu.make_async_copy(state.at[4], theta_out, out_sems.at[0]),
-        pltpu.make_async_copy(state.at[1], momentum_out, out_sems.at[1]),
-    ]
+    last = [store(0, state.at[4]), store(1, state.at[1])]
     start(last)
     for copy in pools:
         copy.wait_send()
     for copy in stores + last:
+        copy.wait()
+
+
+def part_results(result, theta_out, momentum_out, first_out, second_out, sems):
+    outs = (theta_out, momentum_out, first_out, second_out)
+    copies = [pltpu.make_async_copy(result.at[k], out, sems.at[k]) for k, out in enumerate(outs)]
+    for copy in copies:
+        copy.start()
+    for copy in copies:
         copy.wait()
 
 
@@ -292,18 +336,17 @@
     depths, rows = lax.axis_size("replica") // 2, lax.axis_size("shard")
     half, width = block // 2, rows * block
     split = (2, half, head)
-    copies = 2 * (rows + depths - 2)
+    copies = 2 * (rows + depths) + rows
     dma = pltpu.SemaphoreType.DMA
-    anywhere = pl.BlockSpec(memory_space=pl.ANY)
+    in_hbm = pl.BlockSpec(memory_space=pltpu.HBM)
     vmem = pltpu.VMEM
-    outs = pl.pallas_call(
+    result = pl.pallas_call(
         functools.partial(kernel, (steps, depths, rows, islands)),
-        out_shape=[jax.ShapeDtypeStruct(split, F32)] * 4,
-        in_specs=[anywhere] * 6,
-        out_specs=[anywhere] * 4,
+        out_shape=jax.ShapeDtypeStruct((4,) + split, F32),
+        in_specs=[in_hbm] * 6,
+        out_specs=in_hbm,
         scratch_shapes=[
             vmem((steps, depths, 2 * tokens, width), BF16),
-            vmem((steps, depths, width, 2 * tokens), BF16),
             vmem((steps, 2 * tokens, head), BF16),
             vmem((5,) + split, F32),
             vmem((steps, depths, rows) + split, BF16),
@@ -316,21 +359,28 @@
             vmem((steps, rows - 1, depths, half, head), BF16),
             vmem((steps, depths, half, head), BF16),
             vmem((steps, depths - 1, half, head), BF16),
-            vmem(split, F32),
-            vmem((islands - 1,) + split, F32),
+            vmem(split, BF16),
+            vmem((islands - 1,) + split, BF16),
             dma((steps, depths)), dma((steps, depths)), dma((steps, depths)),
-            dma((3,)), dma((4,)), dma((4,)),
+            dma((3,)), dma((4,)),
             dma((steps, 2)), dma((steps, 2)),
             dma((steps, 2, copies)), dma((steps, 2, copies)),
             dma((islands - 1,)), dma((islands - 1,)),
         ],
         compiler_params=pltpu.CompilerParams(
-            collective_id=0, has_side_effects=True, vmem_limit_bytes=40 * 1024 * 1024
+            collective_id=0, has_side_effects=True, vmem_limit_bytes=60 * 1024 * 1024
         ),
     )(
         inputs, targets, theta.reshape(split), momentum.reshape(split),
         first_moment.reshape(split), second_moment.reshape(split),
     )
+    outs = pl.pallas_call(
+        part_results,
+        out_shape=[jax.ShapeDtypeStruct(split, F32)] * 4,
+        in_specs=[in_hbm],
+        out_specs=[in_hbm] * 4,
+        scratch_shapes=[dma((4,))],
+    )(result)
     theta_new, momentum_new, first, second = [out.reshape(block, head) for out in outs]
     return (theta_new, momentum_new, first[None], second[None])
 

time: 89.1 us -> 78 us (0.88)
  local copies, waits for them, and re-layouts: 8.57 us -> 0 us
  Pallas kernels: 79.5 us -> 77.2 us
    unnamed x16 -> x0, local copies, waits for them, and re-layouts: 8.57 us -> none
    pallas_call x1, Pallas kernels: 79.5 us -> 72.1 us  [per_device(): pl.pallas_call(functools.partial(kernel, (steps, depths, rows, islands)),...]
    pallas_call x0 -> x1, Pallas kernels: none -> 5.11 us  [per_device(): pl.pallas_call(part_results, out_shape=[jax.ShapeDtypeStruct(split, F32)]...]
where the time goes in v2:
time: 78 us; the launch traced here: 77.9 us
  Pallas kernels  77.2 us (99%)
    pallas_call x1, Pallas kernels, per_device(): pl.pallas_call(functools.partial(kernel, (steps, depths, rows, islands)),...  72.1 us
    pallas_call x1, Pallas kernels, per_device(): pl.pallas_call(part_results, out_shape=[jax.ShapeDtypeStruct(split, F32)]...  5.11 us

profile of v2, /device:TPU:1, one launch (start us, length us, event | category | flops | bytes accessed | tf_op | source)
XLA Modules:
  0.0 77.9 jit_solution(11581172121961606220)
XLA Ops:
  0.6 72.1 %shard_map.93.result = f32[4,2,32,128]{3,2,1,0:T(8,128)} custom-call(bf16[2,256,4096]{2,1,0:T(8,128)(2,1)} %x_hbm.1, bf16[2,256,128]{2,1,0:T(8,128)(2,1)} %t_hbm.1, f32[2,32,128]{2,1,0:T(8,128)} %bitcast.8, f32[2,32,128]{2,1,0:T(8,128)} %bitcast.9, f32[2,32,128]{2,1,0:T(8,128)} %bitcast.10, f32[2,32,128]{2,1,0:T(8,128)} %bitcast.11), custom_call_target="tpu_custom_call" | custom-call | tf_op jit(solution)/shard_map/pallas_call | solution.py:343
  72.7 5.1 %shard_map.94 = (f32[2,32,128]{2,1,0:T(8,128)}, f32[2,32,128]{2,1,0:T(8,128)}, f32[2,32,128]{2,1,0:T(8,128)}, f32[2,32,128]{2,1,0:T(8,128)}) custom-call(f32[4,2,32,128]{3,2,1,0:T(8,128)} %shard_map.93.result), custom_call_target="tpu_custom_call" | custom-call | tf_op jit(solution)/shard_map/pallas_call | solution.py:377

commit v3 on v2

--- a/solution.py
+++ b/solution.py
@@ -279,11 +279,8 @@
     pools = [pool(k) for k in range(1, islands)]
     start(pools)
 
-    def store(k, source):
-        return pltpu.make_async_copy(source, result.at[k], state_sems.at[k])
-
-    stores = [store(2, state.at[2]), store(3, state.at[3])]
-    start(stores)
+    result[2] = state[2]
+    result[3] = state[3]
     for z in range(depths):
         for s in range(steps):
             x_theirs(s, z).wait_send()
@@ -310,14 +307,10 @@
         total += pool_in[k].astype(F32)
     pseudo_grad = total / islands
     momentum_new = OUTER_MOMENTUM * state[1] + pseudo_grad
-    state[1] = momentum_new
-    state[4] = state[0] - OUTER_RATE * (pseudo_grad + OUTER_MOMENTUM * momentum_new)
-    last = [store(0, state.at[4]), store(1, state.at[1])]
-    start(last)
+    result[1] = momentum_new
+    result[0] = state[0] - OUTER_RATE * (pseudo_grad + OUTER_MOMENTUM * momentum_new)
     for copy in pools:
         copy.wait_send()
-    for copy in stores + last:
-        copy.wait()
 
 
 def part_results(result, theta_out, momentum_out, first_out, second_out, sems):
@@ -339,12 +332,13 @@
     copies = 2 * (rows + depths) + rows
     dma = pltpu.SemaphoreType.DMA
     in_hbm = pl.BlockSpec(memory_space=pltpu.HBM)
+    in_vmem = pl.BlockSpec(memory_space=pltpu.VMEM)
     vmem = pltpu.VMEM
     result = pl.pallas_call(
         functools.partial(kernel, (steps, depths, rows, islands)),
-        out_shape=jax.ShapeDtypeStruct((4,) + split, F32),
+        out_shape=pltpu.VMEM((4,) + split, F32),
         in_specs=[in_hbm] * 6,
-        out_specs=in_hbm,
+        out_specs=in_vmem,
         scratch_shapes=[
             vmem((steps, depths, 2 * tokens, width), BF16),
             vmem((steps, 2 * tokens, head), BF16),
@@ -377,9 +371,10 @@
     outs = pl.pallas_call(
         part_results,
         out_shape=[jax.ShapeDtypeStruct(split, F32)] * 4,
-        in_specs=[in_hbm],
+        in_specs=[in_vmem],
         out_specs=[in_hbm] * 4,
         scratch_shapes=[dma((4,))],
+        compiler_params=pltpu.CompilerParams(vmem_limit_bytes=1024 * 1024),
     )(result)
     theta_new, momentum_new, first, second = [out.reshape(block, head) for out in outs]
     return (theta_new, momentum_new, first[None], second[None])

time: 78 us -> 73 us (0.936)
  Pallas kernels: 77.2 us -> 72.2 us
    pallas_call x1, Pallas kernels: 5.11 us -> 0.68 us  [per_device(): pl.pallas_call(part_results, out_shape=[jax.ShapeDtypeStruct(split, F32)]...]
where the time goes in v3:
time: 73 us; the launch traced here: 72.8 us
  Pallas kernels  72.2 us (99%)
    pallas_call x1, Pallas kernels, per_device(): pl.pallas_call(functools.partial(kernel, (steps, depths, rows, islands)),...  71.5 us

profile of v3, /device:TPU:1, one launch (start us, length us, event | category | flops | bytes accessed | tf_op | source)
XLA Modules:
  0.0 72.8 jit_solution(6449071594773117539)
XLA Ops:
  0.6 71.5 %shard_map.93.result = f32[4,2,32,128]{3,2,1,0:T(8,128)S(1)} custom-call(bf16[2,256,4096]{2,1,0:T(8,128)(2,1)} %x_hbm.1, bf16[2,256,128]{2,1,0:T(8,128)(2,1)} %t_hbm.1, f32[2,32,128]{2,1,0:T(8,128)} %bitcast.8, f32[2,32,128]{2,1,0:T(8,128)} %bitcast.9, f32[2,32,128]{2,1,0:T(8,128)} %bitcast.10, f32[2,32,128]{2,1,0:T(8,128)} %bitcast.11), custom_call_target="tpu_custom_call" | custom-call | tf_op jit(solution)/shard_map/pallas_call | solution.py:337
  72.1 0.7 shard_map.94

commit v4 on v3

v4 whole, which is shorter than its diff:
```python
import functools
import math

import jax
import jax.numpy as jnp
from jax import lax
from jax.experimental import pallas as pl
from jax.experimental.pallas import tpu as pltpu
from jax.sharding import PartitionSpec as P

BETA_ONE = 0.9
BETA_TWO = 0.95
EPSILON = 1e-08
INNER_RATE = 0.05
DECAY = 0.1
OUTER_RATE = 0.7
OUTER_MOMENTUM = 0.9

MESH = pl.DeviceIdType.MESH
F32 = jnp.float32
BF16 = jnp.bfloat16


def far_first(count):
    return sorted(range(1, count), key=lambda k: (-min(k, count - k), k))


def kernel(
    sizes,
    x_hbm, t_hbm, theta_hbm, momentum_hbm, first_hbm, second_hbm,
    result,
    xs, ts, state, weights, part_out, part_in,
    grads, near_a, sum_a, far_a, near_b, sum_b, far_b,
    pool_out, pool_in,
    x_local, x_send, x_recv, t_sems, state_sems,
    part_send, part_recv, send, recv, pool_sems,
):
    steps, depths, rows, islands = sizes
    island = lax.axis_index("island")
    replica = lax.axis_index("replica")
    row = lax.axis_index("shard")
    depth, core = replica // 2, replica % 2
    tokens = x_hbm.shape[1]
    width = xs.shape[3]
    head = t_hbm.shape[2]
    half = weights.shape[3]
    key_scale = (depths * 2 * width) ** (-0.5)
    grad_scale = 1.0 / math.sqrt(tokens * 2 * depths * rows)

    def over_rows(offset):
        return {"shard": (row + offset) % rows}

    def over_depths(offset):
        return {"replica": (depth + offset) % depths * 2 + core}

    sibling = {"replica": depth * 2 + 1 - core}

    def over_islands(offset):
        return {"island": (island + offset) % islands}

    def remote(source, target, send_sem, recv_sem, where):
        return pltpu.make_async_remote_copy(
            src_ref=source, dst_ref=target, send_sem=send_sem, recv_sem=recv_sem,
            device_id=where, device_id_type=MESH,
        )

    barrier = pltpu.get_barrier_semaphore()
    far_rows, far_depths = far_first(rows), far_first(depths)
    near_rows, near_depths = far_rows[::-1], far_depths[::-1]
    outer, inner = far_rows[:3], far_rows[3:]
    greeted = [over_rows(k) for k in far_rows] + [over_depths(k) for k in far_depths]
    greeted += [sibling] + [over_islands(k) for k in range(1, islands)]
    for where in greeted:
        pl.semaphore_signal(barrier, inc=1, device_id=where, device_id_type=MESH)

    def load(k, source):
        return pltpu.make_async_copy(source, state.at[k], state_sems.at[min(k, 1)])

    def loaded(block, sem):
        pltpu.make_async_copy(block, block, sem).wait()

    loads = [load(0, theta_hbm), load(1, momentum_hbm), load(2, first_hbm), load(3, second_hbm)]
    loads[0].start()
    own_tokens = pl.ds(pl.multiple_of(core * tokens, tokens), tokens)

    def x_columns(z, which):
        return pl.ds(pl.multiple_of((z * 2 + which) * width, width), width)

    def x_mine(s, z):
        return pltpu.make_async_copy(
            x_hbm.at[s, :, x_columns(z, core)], xs.at[s, z, own_tokens], x_local.at[s]
        )

    def x_theirs(s, z):
        return remote(
            x_hbm.at[s, :, x_columns(z, 1 - core)], xs.at[s, z, own_tokens],
            x_send.at[0], x_recv.at[s], sibling,
        )

    t_mine = pltpu.make_async_copy(t_hbm, ts.at[:, own_tokens], t_sems.at[0])
    t_theirs = remote(t_hbm, ts.at[:, own_tokens], t_sems.at[1], t_sems.at[2], sibling)
    for z in range(depths):
        x_mine(0, z).start()
    t_mine.start()
    for k in (1, 2, 3):
        loads[k].start()
    for s in range(1, steps):
        for z in range(depths):
            x_mine(s, z).start()

    at_rows, at_depths = 0, rows // 2
    at_a = at_depths + depths // 2
    at_b = at_a + depths - 1
    at_near_a = at_b + depths
    at_near_b = at_near_a + rows
    at_far = at_near_b + depths

    def near_send(s, part, i, where):
        block = weights.at[s, depth * rows + row, part]
        return remote(block, block, send.at[s, 0], recv.at[s, i], where)

    def gather_rows(s, k):
        return near_send(s, 0, at_rows + min(k, rows - k) - 1, over_rows(k))

    def gather_depths(s, k):
        return near_send(s, 1, at_depths + min(k, depths - k) - 1, over_depths(k))

    def received(block, sem):
        remote(block, block, send.at[0, 0], sem, sibling).wait_recv()

    def near_received(s, first, distance, count):
        copies = len({distance, count - distance})
        received(weights.at[s, 0:copies, 0], recv.at[s, first + distance - 1])

    def on_from_row(s, k, targets):
        block = weights.at[s, depth * rows + (row + rows - k) % rows, 0]
        for m in targets:
            remote(block, block, send.at[s, 0], recv.at[s, at_a + m - 1], over_depths(m)).start()

    def on_from_depth(s, k, targets):
        block = weights.at[s, (depth + depths - k) % depths * rows + row, 1]
        for m in targets:
            remote(block, block, send.at[s, 0], recv.at[s, at_b + k], over_rows(m)).start()

    def depth_received(s, k):
        if k > 0:
            received(weights.at[s, 0:rows, 0], recv.at[s, at_a + k - 1])
        received(weights.at[s, 0:rows - 1, 1], recv.at[s, at_b + k])

    def scatter_depths(s, j, k):
        return remote(
            grads.at[s, (depth + k) % depths, (row + j) % rows, 0], near_a.at[s, k - 1, j],
            send.at[s, 1], recv.at[s, at_near_a + j], over_depths(k),
        )

    def scatter_rows(s, j, k):
        return remote(
            grads.at[s, (depth + j) % depths, (row + k) % rows, 1], near_b.at[s, k - 1, j],
            send.at[s, 1], recv.at[s, at_near_b + j], over_rows(k),
        )

    def scatter_far_a(s, k):
        return remote(sum_a.at[s, k], far_a.at[s, k - 1], send.at[s, 1], recv.at[s, at_far], over_rows(k))

    def scatter_far_b(s, k):
        return remote(sum_b.at[s, k], far_b.at[s, k - 1], send.at[s, 1], recv.at[s, at_far + 1], over_depths(k))

    def combine_a(s, j):
        received(near_a.at[s, :, j], recv.at[s, at_near_a + j])
        total = grads[s, depth, (row + j) % rows, 0].astype(F32)
        for k in range(depths - 1):
            total += near_a[s, k, j].astype(F32)
        if j == 0:
            return total
        sum_a[s, j] = total.astype(BF16)
        scatter_far_a(s, j).start()

    def combine_b(s, j):
        received(near_b.at[s, :, j], recv.at[s, at_near_b + j])
        total = grads[s, (depth + j) % depths, row, 1].astype(F32)
        for k in range(rows - 1):
            total += near_b[s, k, j].astype(F32)
        if j == 0:
            return total
        sum_b[s, j] = total.astype(BF16)
        scatter_far_b(s, j).start()

    def gather_start(s, part):
        if part == 0:
            start([gather_rows(s, k) for k in near_rows[:2] + near_rows[6:] + near_rows[2:6]])
        else:
            start([gather_depths(s, k) for k in near_depths])

    def start(copies):
        for copy in copies:
            copy.start()

    def arrive(copies):
        for copy in copies:
            copy.wait_recv()

    near_depth, far_depth = depths > 2, depths // 2
    waits = [(0, 1)] + [(1, 1)] * near_depth + [(0, d) for d in (2, rows // 2, 3) if d < rows // 2 or d == rows // 2 > 1]
    waits = list(dict.fromkeys(waits)) + [(1, far_depth)]

    loads[0].wait()
    weights[0, depth * rows + row] = state[0].astype(BF16)
    pl.semaphore_wait(barrier, len(greeted))
    gather_start(0, 0)
    gather_start(0, 1)

    for s in range(steps):
        on_from_row(s, 0, far_depths)
        on_from_depth(s, 0, far_rows)
        if s == 0:
            for z in range(depths):
                x_theirs(0, z).start()
            t_theirs.start()
        for along, d in waits:
            near_received(s, at_depths if along else at_rows, d, depths if along else rows)
            for k in sorted({d, (depths if along else rows) - d}):
                if along:
                    on_from_depth(s, k, outer)
                else:
                    on_from_row(s, k, far_depths)
        for k in near_depths:
            on_from_depth(s, k, inner)
        if s == 0:
            for later in range(1, steps):
                for z in range(depths):
                    x_theirs(later, z).start()
            t_mine.wait()
            t_theirs.wait_recv()
        loaded(xs.at[s, :, own_tokens], x_local.at[s])
        received(xs.at[s, :, own_tokens], x_recv.at[s])

        def part(p):
            block = part_out.at[s, pl.ds(p * tokens, tokens)]
            return remote(
                block, part_in.at[s, pl.ds(p * tokens, tokens)], part_send.at[0], part_recv.at[s, p], sibling
            )

        for n, k in enumerate([0] + near_depths):
            z = (depth + depths - k) % depths
            depth_received(s, k)
            block = weights[s, pl.ds(z * rows, rows)].reshape(width, head)
            for p in range(2):
                total = jnp.dot(xs[s, z, p * tokens:(p + 1) * tokens], block, preferred_element_type=F32)
                if n > 0:
                    total += part_out[s, p * tokens:(p + 1) * tokens]
                part_out[s, p * tokens:(p + 1) * tokens] = total
                if n == depths - 1:
                    part(p).start()
        arrive([part(0), part(1)])
        projected = (part_out[s] + part_in[s]) * key_scale
        residual = (projected - ts[s].astype(F32)).astype(BF16)

        if s == 0:
            loaded(state.at[1:4], state_sems.at[1])
        for z in far_depths + [0]:
            at = (depth + z) % depths
            gradient = lax.dot_general(
                xs[s, at], residual, (((0,), (0,)), ((), ())), preferred_element_type=F32
            ) * grad_scale
            grads[s, at] = gradient.astype(BF16).reshape(rows, 2, half, head)
            if z > 0:
                start([scatter_depths(s, j, z) for j in outer])
            if z > 0:
                start([scatter_rows(s, z, k) for k in far_rows])
        start([scatter_depths(s, j, z) for j in inner for z in far_depths])
        combine_a(s, far_rows[0])
        start([scatter_rows(s, 0, k) for k in far_rows])
        combine_b(s, far_depths[0])
        start([scatter_depths(s, 0, z) for z in far_depths])
        rest = [(0, j) for j in far_rows[1:3]] + [(1, j) for j in far_depths[1:2]] + [(0, j) for j in far_rows[3:5]]
        rest += [(1, j) for j in far_depths[2:]] + [(0, j) for j in far_rows[5:]]
        for along, j in rest:
            (combine_b if along else combine_a)(s, j)
        totals = {1: combine_b(s, 0), 0: combine_a(s, 0)}

        def update(part_index, gradient):
            parameters = state[0 if s == 0 else 4, part_index]
            first = BETA_ONE * state[2, part_index] + (1.0 - BETA_ONE) * gradient
            second = BETA_TWO * state[3, part_index] + (1.0 - BETA_TWO) * gradient * gradient
            parameters = parameters - INNER_RATE * (
                first / (jnp.sqrt(second) + EPSILON) + DECAY * parameters
            )
            state[2, part_index] = first
            state[3, part_index] = second
            state[4, part_index] = parameters
            if s < steps - 1:
                weights[s + 1, depth * rows + row, part_index] = parameters.astype(BF16)
                gather_start(s + 1, part_index)

        received(far_a.at[s], recv.at[s, at_far])
        for k in range(rows - 1):
            totals[0] += far_a[s, k].astype(F32)
        update(0, totals[0])
        received(far_b.at[s], recv.at[s, at_far + 1])
        for k in range(depths - 1):
            totals[1] += far_b[s, k].astype(F32)
        update(1, totals[1])

    moved = state[0] - state[4]
    pool_out[...] = moved.astype(BF16)

    def pool(k):
        return remote(
            pool_out, pool_in.at[k - 1], pool_sems.at[0], pool_sems.at[1], over_islands(k)
        )

    pools = [pool(k) for k in range(1, islands)]
    start(pools)

    result[2] = state[2]
    result[3] = state[3]
    def left(block, sem):
        remote(block, block, sem, x_recv.at[0], sibling).wait_send()

    left(xs.at[:, :, own_tokens], x_send.at[0])
    left(ts.at[:, own_tokens], t_sems.at[1])
    left(part_out, part_send.at[0])
    for s in range(steps):
        for sem in (send.at[s, 0], send.at[s, 1]):
            left(weights.at[s, 0:depths * rows - 1], sem)
    received(pool_in, pool_sems.at[1])
    total = moved
    for k in range(islands - 1):
        total += pool_in[k].astype(F32)
    pseudo_grad = total / islands
    momentum_new = OUTER_MOMENTUM * state[1] + pseudo_grad
    result[1] = momentum_new
    result[0] = state[0] - OUTER_RATE * (pseudo_grad + OUTER_MOMENTUM * momentum_new)
    left(pool_in, pool_sems.at[0])


def part_results(result, theta_out, momentum_out, first_out, second_out, sems):
    outs = (theta_out, momentum_out, first_out, second_out)
    copies = [pltpu.make_async_copy(result.at[k], out, sems.at[k]) for k, out in enumerate(outs)]
    for copy in copies:
        copy.start()
    for copy in copies:
        copy.wait()


def per_device(inputs, targets, theta, momentum, first_moment, second_moment):
    steps, tokens, _ = inputs.shape
    block, head = theta.shape
    islands = lax.axis_size("island")
    depths, rows = lax.axis_size("replica") // 2, lax.axis_size("shard")
    half, width = block // 2, rows * block
    split = (2, half, head)
    arrivals = rows // 2 + depths // 2 + depths - 1 + depths + rows + depths + 2
    dma = pltpu.SemaphoreType.DMA
    in_hbm = pl.BlockSpec(memory_space=pltpu.HBM)
    in_vmem = pl.BlockSpec(memory_space=pltpu.VMEM)
    vmem = pltpu.VMEM
    result = pl.pallas_call(
        functools.partial(kernel, (steps, depths, rows, islands)),
        out_shape=pltpu.VMEM((4,) + split, F32),
        in_specs=[in_hbm] * 6,
        out_specs=in_vmem,
        scratch_shapes=[
            vmem((steps, depths, 2 * tokens, width), BF16),
            vmem((steps, 2 * tokens, head), BF16),
            vmem((5,) + split, F32),
            vmem((steps, depths * rows) + split, BF16),
            vmem((steps, 2 * tokens, head), F32),
            vmem((steps, 2 * tokens, head), F32),
            vmem((steps, depths, rows) + split, BF16),
            vmem((steps, depths - 1, rows, half, head), BF16),
            vmem((steps, rows, half, head), BF16),
            vmem((steps, rows - 1, half, head), BF16),
            vmem((steps, rows - 1, depths, half, head), BF16),
            vmem((steps, depths, half, head), BF16),
            vmem((steps, depths - 1, half, head), BF16),
            vmem(split, BF16),
            vmem((islands - 1,) + split, BF16),
            dma((steps,)), dma((1,)), dma((steps,)),
            dma((3,)), dma((2,)),
            dma((1,)), dma((steps, 2)),
            dma((steps, 2)), dma((steps, arrivals)),
            dma((2,)),
        ],
        compiler_params=pltpu.CompilerParams(
            collective_id=0, has_side_effects=True, vmem_limit_bytes=60 * 1024 * 1024
        ),
    )(
        inputs, targets, theta.reshape(split), momentum.reshape(split),
        first_moment.reshape(split), second_moment.reshape(split),
    )
    outs = pl.pallas_call(
        part_results,
        out_shape=[jax.ShapeDtypeStruct(split, F32)] * 4,
        in_specs=[in_vmem],
        out_specs=[in_hbm] * 4,
        scratch_shapes=[dma((4,))],
        compiler_params=pltpu.CompilerParams(vmem_limit_bytes=1024 * 1024),
    )(result)
    theta_new, momentum_new, first, second = [out.reshape(block, head) for out in outs]
    return (theta_new, momentum_new, first[None], second[None])


def solution(mesh):
    in_specs = (
        P(None, ("island", "replica", "shard"), None),
        P(None, ("island", "replica", "shard"), None),
        P(("replica", "shard"), None),
        P(("replica", "shard"), None),
        P("island", ("replica", "shard"), None),
        P("island", ("replica", "shard"), None),
    )
    out_specs = (
        P(("replica", "shard"), None),
        P(("replica", "shard"), None),
        P("island", ("replica", "shard"), None),
        P("island", ("replica", "shard"), None),
    )
    return jax.shard_map(
        per_device, mesh=mesh, in_specs=in_specs, out_specs=out_specs, check_vma=False
    )
```

time: 73 us -> 68.4 us (0.937)
  Pallas kernels: 72.2 us -> 67.6 us
    pallas_call x1, Pallas kernels: 71.5 us -> 66.9 us  [per_device(): pl.pallas_call(functools.partial(kernel, (steps, depths, rows, islands)),...]
where the time goes in v4:
time: 68.4 us; the launch traced here: 68.2 us
  Pallas kernels  67.6 us (99%)
    pallas_call x1, Pallas kernels, per_device(): pl.pallas_call(functools.partial(kernel, (steps, depths, rows, islands)),...  66.9 us

profile of v4, /device:TPU:1, one launch (start us, length us, event | category | flops | bytes accessed | tf_op | source)
XLA Modules:
  0.0 68.2 jit_solution(4488821090717432274)
XLA Ops:
  0.6 66.9 %shard_map.93.result = f32[4,2,32,128]{3,2,1,0:T(8,128)S(1)} custom-call(bf16[2,256,4096]{2,1,0:T(8,128)(2,1)} %x_hbm.1, bf16[2,256,128]{2,1,0:T(8,128)(2,1)} %t_hbm.1, f32[2,32,128]{2,1,0:T(8,128)} %bitcast.8, f32[2,32,128]{2,1,0:T(8,128)} %bitcast.9, f32[2,32,128]{2,1,0:T(8,128)} %bitcast.10, f32[2,32,128]{2,1,0:T(8,128)} %bitcast.11), custom_call_target="tpu_custom_call" | custom-call | tf_op jit(solution)/shard_map/pallas_call | solution.py:358
  67.5 0.7 %shard_map.94 = (f32[2,32,128]{2,1,0:T(8,128)}, f32[2,32,128]{2,1,0:T(8,128)}, f32[2,32,128]{2,1,0:T(8,128)}, f32[2,32,128]{2,1,0:T(8,128)}) custom-call(f32[4,2,32,128]{3,2,1,0:T(8,128)S(1)} %shard_map.93.result), custom_call_target="tpu_custom_call" | custom-call | tf_op jit(solution)/shard_map/pallas_call | solution.py:392

commit v5 on v4

--- a/solution.py
+++ b/solution.py
@@ -117,7 +117,7 @@
 
     def near_send(s, part, i, where):
         block = weights.at[s, depth * rows + row, part]
-        return remote(block, block, send.at[s, 0], recv.at[s, i], where)
+        return remote(block, block, send.at[0], recv.at[0, i], where)
 
     def gather_rows(s, k):
         return near_send(s, 0, at_rows + min(k, rows - k) - 1, over_rows(k))
@@ -126,47 +126,47 @@
         return near_send(s, 1, at_depths + min(k, depths - k) - 1, over_depths(k))
 
     def received(block, sem):
-        remote(block, block, send.at[0, 0], sem, sibling).wait_recv()
+        remote(block, block, send.at[0], sem, sibling).wait_recv()
 
     def near_received(s, first, distance, count):
         copies = len({distance, count - distance})
-        received(weights.at[s, 0:copies, 0], recv.at[s, first + distance - 1])
+        received(weights.at[s, 0:copies, 0], recv.at[0, first + distance - 1])
 
     def on_from_row(s, k, targets):
         block = weights.at[s, depth * rows + (row + rows - k) % rows, 0]
         for m in targets:
-            remote(block, block, send.at[s, 0], recv.at[s, at_a + m - 1], over_depths(m)).start()
+            remote(block, block, send.at[0], recv.at[0, at_a + m - 1], over_depths(m)).start()
 
     def on_from_depth(s, k, targets):
         block = weights.at[s, (depth + depths - k) % depths * rows + row, 1]
         for m in targets:
-            remote(block, block, send.at[s, 0], recv.at[s, at_b + k], over_rows(m)).start()
+            remote(block, block, send.at[0], recv.at[0, at_b + k], over_rows(m)).start()
 
     def depth_received(s, k):
         if k > 0:
-            received(weights.at[s, 0:rows, 0], recv.at[s, at_a + k - 1])
-        received(weights.at[s, 0:rows - 1, 1], recv.at[s, at_b + k])
+            received(weights.at[s, 0:rows, 0], recv.at[0, at_a + k - 1])
+        received(weights.at[s, 0:rows - 1, 1], recv.at[0, at_b + k])
 
     def scatter_depths(s, j, k):
         return remote(
             grads.at[s, (depth + k) % depths, (row + j) % rows, 0], near_a.at[s, k - 1, j],
-            send.at[s, 1], recv.at[s, at_near_a + j], over_depths(k),
+            send.at[1], recv.at[0, at_near_a + j], over_depths(k),
         )
 
     def scatter_rows(s, j, k):
         return remote(
             grads.at[s, (depth + j) % depths, (row + k) % rows, 1], near_b.at[s, k - 1, j],
-            send.at[s, 1], recv.at[s, at_near_b + j], over_rows(k),
+            send.at[1], recv.at[0, at_near_b + j], over_rows(k),
         )
 
     def scatter_far_a(s, k):
-        return remote(sum_a.at[s, k], far_a.at[s, k - 1], send.at[s, 1], recv.at[s, at_far], over_rows(k))
+        return remote(sum_a.at[s, k], far_a.at[s, k - 1], send.at[1], recv.at[0, at_far], over_rows(k))
 
     def scatter_far_b(s, k):
-        return remote(sum_b.at[s, k], far_b.at[s, k - 1], send.at[s, 1], recv.at[s, at_far + 1], over_depths(k))
+        return remote(sum_b.at[s, k], far_b.at[s, k - 1], send.at[1], recv.at[0, at_far + 1], over_depths(k))
 
     def combine_a(s, j):
-        received(near_a.at[s, :, j], recv.at[s, at_near_a + j])
+        received(near_a.at[s, :, j], recv.at[0, at_near_a + j])
         total = grads[s, depth, (row + j) % rows, 0].astype(F32)
         for k in range(depths - 1):
             total += near_a[s, k, j].astype(F32)
@@ -176,7 +176,7 @@
         scatter_far_a(s, j).start()
 
     def combine_b(s, j):
-        received(near_b.at[s, :, j], recv.at[s, at_near_b + j])
+        received(near_b.at[s, :, j], recv.at[0, at_near_b + j])
         total = grads[s, (depth + j) % depths, row, 1].astype(F32)
         for k in range(rows - 1):
             total += near_b[s, k, j].astype(F32)
@@ -292,14 +292,14 @@
                 weights[s + 1, depth * rows + row, part_index] = parameters.astype(BF16)
                 gather_start(s + 1, part_index)
 
-        received(far_a.at[s], recv.at[s, at_far])
+        received(far_b.at[s], recv.at[0, at_far + 1])
+        for k in range(depths - 1):
+            totals[1] += far_b[s, k].astype(F32)
+        update(1, totals[1])
+        received(far_a.at[s], recv.at[0, at_far])
         for k in range(rows - 1):
             totals[0] += far_a[s, k].astype(F32)
         update(0, totals[0])
-        received(far_b.at[s], recv.at[s, at_far + 1])
-        for k in range(depths - 1):
-            totals[1] += far_b[s, k].astype(F32)
-        update(1, totals[1])
 
     moved = state[0] - state[4]
     pool_out[...] = moved.astype(BF16)
@@ -309,7 +309,7 @@
             pool_out, pool_in.at[k - 1], pool_sems.at[0], pool_sems.at[1], over_islands(k)
         )
 
-    pools = [pool(k) for k in range(1, islands)]
+    pools = [pool(k) for k in sorted(range(1, islands), key=lambda k: -min(k % 4, 4 - k % 4))]
     start(pools)
 
     result[2] = state[2]
@@ -320,9 +320,8 @@
     left(xs.at[:, :, own_tokens], x_send.at[0])
     left(ts.at[:, own_tokens], t_sems.at[1])
     left(part_out, part_send.at[0])
-    for s in range(steps):
-        for sem in (send.at[s, 0], send.at[s, 1]):
-            left(weights.at[s, 0:depths * rows - 1], sem)
+    for k in range(2):
+        left(weights.at[:, 0:depths * rows - 1], send.at[k])
     received(pool_in, pool_sems.at[1])
     total = moved
     for k in range(islands - 1):
@@ -379,7 +378,7 @@
             dma((steps,)), dma((1,)), dma((steps,)),
             dma((3,)), dma((2,)),
             dma((1,)), dma((steps, 2)),
-            dma((steps, 2)), dma((steps, arrivals)),
+            dma((2,)), dma((1, arrivals)),
             dma((2,)),
         ],
         compiler_params=pltpu.CompilerParams(

time: 68.4 us -> 68 us (level)
  no operation moved by 1% of the time
where the time goes in v5:
time: 68 us; the launch traced here: 67.8 us
  Pallas kernels  67.2 us (99%)
    pallas_call x1, Pallas kernels, per_device(): pl.pallas_call(functools.partial(kernel, (steps, depths, rows, islands)),...  66.5 us

profile of v5, /device:TPU:1, one launch (start us, length us, event | category | flops | bytes accessed | tf_op | source)
XLA Modules:
  0.0 67.8 jit_solution(765191138889141063)
XLA Ops:
  0.6 66.5 %shard_map.93.result = f32[4,2,32,128]{3,2,1,0:T(8,128)S(1)} custom-call(bf16[2,256,4096]{2,1,0:T(8,128)(2,1)} %x_hbm.1, bf16[2,256,128]{2,1,0:T(8,128)(2,1)} %t_hbm.1, f32[2,32,128]{2,1,0:T(8,128)} %bitcast.8, f32[2,32,128]{2,1,0:T(8,128)} %bitcast.9, f32[2,32,128]{2,1,0:T(8,128)} %bitcast.10, f32[2,32,128]{2,1,0:T(8,128)} %bitcast.11), custom_call_target="tpu_custom_call" | custom-call | tf_op jit(solution)/shard_map/pallas_call | solution.py:357
  67.1 0.7 %shard_map.94 = (f32[2,32,128]{2,1,0:T(8,128)}, f32[2,32,128]{2,1,0:T(8,128)}, f32[2,32,128]{2,1,0:T(8,128)}, f32[2,32,128]{2,1,0:T(8,128)}) custom-call(f32[4,2,32,128]{3,2,1,0:T(8,128)S(1)} %shard_map.93.result), custom_call_target="tpu_custom_call" | custom-call | tf_op jit(solution)/shard_map/pallas_call | solution.py:391
